TPU v7x, 256 devices: a whole 4x4x8 slice. The times are simulated.
256 devices in a mesh: sub: 16 (over z, core), row: 16 (over y, x).
Axes of the slice: x: 4, y: 4, z: 8, core: 2. Of those that a mesh axis runs over, the one named last changes fastest.
Arguments:
- modes: float32 [196608, 64], P(('sub', 'row')), may hold values from -6 to 6
- search: float32 [196608, 64], P(('sub', 'row')), may hold values from -6 to 6
- precond: float32 [196608], P(('sub', 'row')), may hold values from 0.05 to 0.25
- in_row: int32 [16, 16, 96], P('sub', 'row'), may hold values from 0 to 11, as said below
- in_col: int32 [16, 16, 96], P('sub', 'row'), may hold values from 0 to 191, as said below
- in_val: bfloat16 [16, 16, 96, 64, 64], P('sub', 'row'), as said below
- bnd_rows: int32 [16, 16, 3], P('sub', 'row'), may hold values from 0 to 11, as said below
- if_row: int32 [16, 16, 12], P('sub', 'row'), may hold values from 0 to 11, as said below
- if_src: int32 [16, 16, 12], P('sub', 'row'), may hold values from 0 to 47, as said below
- if_val: bfloat16 [16, 16, 12, 64, 64], P('sub', 'row')
Outputs:
- modes_out: float32 [196608, 64], P(('sub', 'row'))
- search_out: float32 [196608, 64], P(('sub', 'row'))
Inputs may be any that keep to these rules, and one draw needn't show every extreme that they name: `in_row`: entry k < 12 is k; each later group of 12 entries names each of the device's block-rows once. `in_col`: entry k < 12 is r * 12 + k on device (s, r); in each later group of 12 entries the devices of a subdomain together name each of its 192 block-rows once, and no entry names its own block-row. `in_val`: the first 12 blocks of every device are symmetric; the operator A is symmetric positive definite. `bnd_rows`: distinct within a device. `if_row`: each of the device's 12 block-rows once. `if_src`: t * 3 + q with t never the device's own subdomain; among the devices with one index of row, each boundary slot of each subdomain is named exactly 4 times.
All inputs are finite; a program needn't handle non-finite values.
Results may differ from a plain program's by a relative error of at most 0.0006.
Values may be sent and summed in bfloat16 or wider, within the bound.
A program may use at most 128 MiB of HBM per device.

v0:
```python
import jax
import jax.numpy as jnp
from jax import lax
from jax.sharding import PartitionSpec as P

KB = 64
LB = 12
ITERS = 2
IFR = 3
precise_mode = lax.Precision.HIGHEST


def gram_product(left, right):
    return jnp.dot(left.T, right, precision=precise_mode, preferred_element_type=jnp.float32)


def full_dot(left, right):
    return jnp.dot(left, right, precision=precise_mode, preferred_element_type=jnp.float32)


def chol_solve(matrix, rhs):
    factor = jnp.linalg.cholesky(matrix)
    halfway = lax.linalg.triangular_solve(factor, rhs, left_side=True, lower=True)
    return lax.linalg.triangular_solve(
        factor, halfway, left_side=True, lower=True, transpose_a=True
    )


def rescale(factor, moved):
    return lax.linalg.triangular_solve(factor, moved, left_side=False, lower=True, transpose_a=True)


def project(current, image_x):
    return lax.psum(
        (gram_product(current, current), gram_product(current, image_x)), ("sub", "row")
    )


def apply_blocks(vector, blocks):
    rows_here, cols_here, vals_here, bnd_here, face_rows, face_src, face_vals = blocks
    width = vector.shape[1]
    mine = vector.reshape(LB, KB, width)
    local_ids = jnp.arange(LB, dtype=jnp.int32)
    position = lax.axis_index("row")
    group = lax.all_gather(vector, "row", axis=0, tiled=True).reshape(-1, KB, width)
    forward = jnp.einsum("kij,kjw->kiw", vals_here, group[cols_here], precision=precise_mode)
    select = (rows_here[:, None] == local_ids[None, :]).astype(jnp.float32)
    result = jnp.einsum("ka,kiw->aiw", select, forward, precision=precise_mode)
    backward = jnp.einsum("kji,kjw->kiw", vals_here, mine[rows_here], precision=precise_mode)
    keeper = (cols_here != position * LB + rows_here).astype(jnp.float32)
    backward = backward * keeper[:, None, None]
    wanted = jnp.arange(LB * KB * lax.axis_size("row") // KB, dtype=jnp.int32)
    chosen = (cols_here[None, :] == wanted[:, None]).astype(jnp.float32)
    returned = lax.psum_scatter(
        jnp.einsum("bk,kiw->biw", chosen, backward, precision=precise_mode).reshape(
            LB * KB * lax.axis_size("row"), width
        ),
        "row",
        scatter_dimension=0,
        tiled=True,
    )
    result = result + returned.reshape(LB, KB, width)
    boundary = mine[bnd_here].reshape(-1, width)
    remote = lax.all_gather(boundary, "sub", axis=0, tiled=True).reshape(-1, KB, width)
    forward = jnp.einsum("kij,kjw->kiw", face_vals, remote[face_src], precision=precise_mode)
    face_select = (face_rows[:, None] == local_ids[None, :]).astype(jnp.float32)
    result = result + jnp.einsum("ka,kiw->aiw", face_select, forward, precision=precise_mode)
    backward = jnp.einsum("kji,kjw->kiw", face_vals, mine[face_rows], precision=precise_mode)
    wanted = jnp.arange(IFR * KB * lax.axis_size("sub") // KB, dtype=jnp.int32)
    chosen = (face_src[None, :] == wanted[:, None]).astype(jnp.float32)
    landed = lax.psum_scatter(
        jnp.einsum("bk,kiw->biw", chosen, backward, precision=precise_mode).reshape(
            IFR * KB * lax.axis_size("sub"), width
        ),
        "sub",
        scatter_dimension=0,
        tiled=True,
    ).reshape(IFR, KB, width)
    placed = (bnd_here[:, None] == local_ids[None, :]).astype(jnp.float32)
    result = result + jnp.einsum("qa,qiw->aiw", placed, landed, precision=precise_mode)
    return result.reshape(LB * KB, width)


def local(modes, search, precond, in_row, in_col, in_val, bnd_rows, if_row, if_src, if_val):
    blocks = (
        in_row[0, 0],
        in_col[0, 0],
        in_val[0, 0].astype(jnp.float32),
        bnd_rows[0, 0],
        if_row[0, 0],
        if_src[0, 0],
        if_val[0, 0].astype(jnp.float32),
    )
    total_rows = modes.shape[0] * lax.axis_size("sub") * lax.axis_size("row")
    nmode = modes.shape[1]
    images = apply_blocks(jnp.concatenate([modes, search], 1), blocks)
    current, direction = (modes, search)
    image_x, image_p = (images[:, :nmode], images[:, nmode:])
    for sweep in range(ITERS):
        correlation, energy = project(current, image_x)
        ritz = chol_solve(correlation, energy)
        residue = image_x - full_dot(current, ritz)
        update = precond[:, None] * residue
        image_w = apply_blocks(update, blocks)
        basis = jnp.concatenate([update, direction], 1)
        image_b = jnp.concatenate([image_w, image_p], 1)
        coupled, driving = lax.psum(
            (gram_product(basis, image_b), gram_product(basis, image_x)), ("sub", "row")
        )
        coeffs = -chol_solve(coupled, driving)
        step_x = full_dot(basis, coeffs)
        step_a = full_dot(image_b, coeffs)
        moved = current + step_x
        moved_image = image_x + step_a
        lengths = lax.psum(gram_product(moved, moved), ("sub", "row"))
        factor = jnp.linalg.cholesky(lengths / total_rows)
        current = rescale(factor, moved)
        image_x = rescale(factor, moved_image)
        direction = rescale(factor, step_x)
        image_p = rescale(factor, step_a)
    return (current, direction)


def solution(mesh):
    return jax.shard_map(
        local,
        mesh=mesh,
        in_specs=(
            P(("sub", "row"), None),
            P(("sub", "row"), None),
            P(("sub", "row")),
            P("sub", "row", None),
            P("sub", "row", None),
            P("sub", "row", None, None, None),
            P("sub", "row", None),
            P("sub", "row", None),
            P("sub", "row", None),
            P("sub", "row", None, None, None),
        ),
        out_specs=(P(("sub", "row"), None), P(("sub", "row"), None)),
        check_vma=False,
    )
```

profile of v0, /device:TPU:1, one launch (start us, length us, event | category | flops | bytes accessed | tf_op | source)
XLA Modules:
  0.0 1590.2 jit_solution(9537704448237477838)
XLA Ops:
  30.9 6.3 copy.146
  41.8 13.2 all-gather.9.cloned.1.call-done
  57.4 53.8 %reduce-scatter.13.cloned.1.call-done = f32[192,128]{1,0:T(8,128)} async-done(((f32[3072,128]{1,0:T(8,128)}), f32[192,128]{1,0:T(8,128)}) %reduce-scatter.13.cloned.1.call-update) | async-done | bytes 98320 | tf_op jit(solution)/shard_map/reduce_scatter | solution.py:71
  112.6 69.1 %all-gather.7.cloned.1.call-done = f32[12288,128]{1,0:T(8,128)} async-done(((f32[768,128]{1,0:T(8,128)}), f32[12288,128]{1,0:T(8,128)}) %all-gather.7.cloned.1.call-update) | async-done | bytes 6291472 | tf_op jit(solution)/shard_map/all_gather | solution.py:45
  181.7 5.2 gather_fusion
  186.9 5.3 convolution_bitcast_fusion.2
  192.2 78.6 %reduce-scatter.11.cloned.1.call-done = f32[768,128]{1,0:T(8,128)} async-done(((f32[12288,128]{1,0:T(8,128)}), f32[768,128]{1,0:T(8,128)}) %reduce-scatter.11.cloned.1.call-update) | async-done | bytes 393232 | tf_op jit(solution)/shard_map/reduce_scatter | solution.py:54
  270.8 4.8 fusion.7
  277.3 76.9 %all-reduce.1 = (f32[64,64]{0,1:T(8,128)S(1)}, f32[64,64]{0,1:T(8,128)S(1)}) all-reduce(f32[64,64]{0,1:T(8,128)S(1)} %convolution_bitcast_fusion.16, f32[64,64]{0,1:T(8,128)} %fusion.130), channel_id=1, replica_groups=mesh['sub'=16,'row'=16] {'sub','row'}, use_global_device_ids=true, to_apply=%region_5.0 | all-reduce | flops 8192 | bytes 65536 | tf_op jit(solution)/shard_map/psum | solution.py:34
  354.3 5.8 cholesky.116
  361.5 4.9 custom-call.29
  381.2 6.5 multiply_bitcast_fusion.1
  392.4 5.5 fusion.44
  397.9 6.3 copy.165
  404.2 5.9 reshape.293
  411.0 21.9 %all-gather = f32[16,192,64]{1,2,0:T(8,128)} all-gather(f32[1,192,64]{1,2,0:T(8,128)S(1)} %copy.168), channel_id=1, replica_groups=mesh['sub'=16,'row'=16] {'sub'}, dimensions={0}, use_global_device_ids=true | all-gather | bytes 835584 | tf_op jit(solution)/shard_map/all_gather | solution.py:64
  441.7 45.4 %all-gather.11.cloned.1.call-done = f32[12288,64]{0,1:T(8,128)} async-done(((f32[768,64]{0,1:T(8,128)}), f32[12288,64]{0,1:T(8,128)}) %all-gather.11.cloned.1.call-update) | async-done | bytes 3145744 | tf_op jit(solution)/shard_map/all_gather | solution.py:45
  487.1 5.8 copy.233
  492.8 5.3 gather_fusion.5
  498.1 6.2 convolution_bitcast_fusion.1
  509.1 60.1 %reduce-scatter.15.cloned.1.call-done = f32[768,64]{0,1:T(8,128)} async-done(((f32[12288,64]{0,1:T(8,128)}), f32[768,64]{0,1:T(8,128)}) %reduce-scatter.15.cloned.1.call-update) | async-done | bytes 196624 | tf_op jit(solution)/shard_map/reduce_scatter | solution.py:54
  582.2 77.9 %psum.73 = f32[128,64]{0,1:T(8,128)S(1)} all-reduce(f32[128,64]{0,1:T(8,128)} %fusion.27), channel_id=1, replica_groups=mesh['sub'=16,'row'=16] {'sub','row'}, use_global_device_ids=true, to_apply=%region_11.16 | all-reduce | flops 8192 | bytes 65536 | tf_op jit(solution)/shard_map/psum | solution.py:107
  660.1 160.0 %all-reduce.5.cloned.1.call-done = f32[128,128]{0,1:T(8,128)} async-done(((f32[128,128]{0,1:T(8,128)}), f32[128,128]{0,1:T(8,128)}) %all-reduce.5.cloned.1.call-update) | async-done | bytes 65552 | tf_op jit(solution)/shard_map/psum | solution.py:107
  821.9 11.7 cholesky.127
  835.0 9.8 custom-call.31
  847.9 74.6 %psum.74 = f32[64,64]{0,1:T(8,128)S(1)} all-reduce(f32[64,64]{0,1:T(8,128)S(1)} %fusion.131), channel_id=1, replica_groups=mesh['sub'=16,'row'=16] {'sub','row'}, use_global_device_ids=true, to_apply=%region_12.19 | all-reduce | flops 4096 | bytes 32768 | tf_op jit(solution)/shard_map/psum | solution.py:115
  922.5 5.8 cholesky.138
  929.7 4.9 custom-call.32
  937.0 74.2 %all-reduce = (f32[64,64]{1,0:T(8,128)S(1)}, f32[64,64]{0,1:T(8,128)S(1)}) all-reduce(f32[64,64]{1,0:T(8,128)S(1)} %fusion.133, f32[64,64]{0,1:T(8,128)S(1)} %fusion.132), channel_id=1, replica_groups=mesh['sub'=16,'row'=16] {'sub','row'}, use_global_device_ids=true, to_apply=%region_14.22 | all-reduce | flops 8192 | bytes 65536 | tf_op jit(solution)/shard_map/psum | solution.py:34
  1011.3 5.8 cholesky.149
  1018.5 4.9 custom-call.35
  1034.0 6.6 multiply_bitcast_fusion
  1045.2 5.5 fusion.43
  1050.7 6.3 copy.195
  1057.0 5.9 reshape.302
  1063.8 19.7 %all-gather.1 = f32[16,192,64]{1,2,0:T(8,128)S(1)} all-gather(f32[1,192,64]{1,2,0:T(8,128)S(1)} %copy.198), channel_id=1, replica_groups=mesh['sub'=16,'row'=16] {'sub'}, dimensions={0}, use_global_device_ids=true | all-gather | bytes 835584 | tf_op jit(solution)/shard_map/all_gather | solution.py:64
  1091.1 47.1 %all-gather.13.cloned.1.call-done = f32[12288,64]{0,1:T(8,128)} async-done(((f32[768,64]{0,1:T(8,128)}), f32[12288,64]{0,1:T(8,128)}) %all-gather.13.cloned.1.call-update) | async-done | bytes 3145744 | tf_op jit(solution)/shard_map/all_gather | solution.py:45
  1138.2 5.8 copy.237
  1143.9 5.3 gather_fusion.10
  1149.2 6.2 convolution_bitcast_fusion
  1160.1 60.5 %reduce-scatter.17.cloned.1.call-done = f32[768,64]{0,1:T(8,128)} async-done(((f32[12288,64]{0,1:T(8,128)}), f32[768,64]{0,1:T(8,128)}) %reduce-scatter.17.cloned.1.call-update) | async-done | bytes 196624 | tf_op jit(solution)/shard_map/reduce_scatter | solution.py:54
  1229.7 77.7 %psum.78 = f32[128,64]{0,1:T(8,128)S(1)} all-reduce(f32[128,64]{0,1:T(8,128)S(1)} %fusion.25), channel_id=1, replica_groups=mesh['sub'=16,'row'=16] {'sub','row'}, use_global_device_ids=true, to_apply=%region_18.26 | all-reduce | flops 8192 | bytes 65536 | tf_op jit(solution)/shard_map/psum | solution.py:107
  1307.4 161.1 %all-reduce.7.cloned.1.call-done = f32[128,128]{0,1:T(8,128)} async-done(((f32[128,128]{0,1:T(8,128)}), f32[128,128]{0,1:T(8,128)}) %all-reduce.7.cloned.1.call-update) | async-done | bytes 65552 | tf_op jit(solution)/shard_map/psum | solution.py:107
  1470.3 11.7 cholesky.160
  1483.3 9.8 custom-call.39
  1494.3 74.6 %psum.79 = f32[64,64]{0,1:T(8,128)S(1)} all-reduce(f32[64,64]{0,1:T(8,128)S(1)} %fusion.134), channel_id=1, replica_groups=mesh['sub'=16,'row'=16] {'sub','row'}, use_global_device_ids=true, to_apply=%region_19.27 | all-reduce | flops 4096 | bytes 32768 | tf_op jit(solution)/shard_map/psum | solution.py:115
  1569.0 5.8 cholesky.171
  1576.1 4.9 custom-call.40
  (221 shorter events, 137.8 us)
Async XLA Ops:
  7.2 5.7 copy-start
  7.2 6.1 copy-start.24
  7.2 47.9 %all-gather.9.cloned.1.call-start = ((), (), s32[]{:S(2)}) async-start(), calls=%async_computation.8 | async-start | bytes 1671168 | tf_op jit(solution)/shard_map/all_gather | solution.py:64
  10.1 5.7 copy-start.19
  10.3 5.5 copy-start.1
  11.5 99.6 %reduce-scatter.13.cloned.1.call-start = ((), (), s32[]{:S(2)}) async-start(), calls=%async_computation.9 | async-start | bytes 1671168 | tf_op jit(solution)/shard_map/reduce_scatter | solution.py:71
  12.3 3.6 copy-start.22
  13.2 3.9 copy-start.18
  15.8 1.4 copy-start.2
  15.9 165.8 %all-gather.7.cloned.1.call-start = ((), (), s32[]{:S(2)}) async-start(), calls=%async_computation.6 | async-start | bytes 6684672 | tf_op jit(solution)/shard_map/all_gather | solution.py:45
  16.6 254.2 %reduce-scatter.11.cloned.1.call-start = ((), (), s32[]{:S(2)}) async-start(), calls=%async_computation.7 | async-start | bytes 6684672 | tf_op jit(solution)/shard_map/reduce_scatter | solution.py:54
  17.2 2.5 copy-start.21
  17.2 2.5 copy-start.8
  17.2 5.3 copy-start.16
  37.2 3.6 copy-start.3
  37.3 73.9 %copy-start.29 = (s32[1,1,3]{2,1,0:T(1,128)S(1)}, s32[1,1,3]{2,1,0:T(1,128)}, u32[]{:S(2)}) copy-start(s32[1,1,3]{2,1,0:T(1,128)} %param.28) | copy-start | bytes 40
  37.3 402.2 %reduce-scatter.19.cloned.1.call-start = ((), (), s32[]{:S(2)}) async-start(), calls=%async_computation.16 | async-start | bytes 1671168 | tf_op jit(solution)/shard_map/reduce_scatter | solution.py:71
  40.8 146.0 %copy-start.20 = (s32[1024]{0:T(1024)}, s32[1024]{0:T(1024)S(1)}, u32[]{:S(2)}) copy-start(s32[1024]{0:T(1024)S(1)} %pad_clamp_fusion.4) | copy-start | bytes 12292
  40.9 14.2 copy-start.23
  192.2 83.4 %copy-start.26 = (s32[1,1,12]{2,1,0:T(1,128)S(1)}, s32[1,1,12]{2,1,0:T(1,128)}, u32[]{:S(2)}) copy-start(s32[1,1,12]{2,1,0:T(1,128)} %param.29) | copy-start | bytes 148
  275.6 92.0 %copy-start.17 = (f32[768]{0:T(1024)S(1)}, f32[768]{0:T(1024)}, u32[]{:S(2)}) copy-start(f32[768]{0:T(1024)} %param.24) | copy-start | bytes 9220
  367.6 10.2 copy-start.13
  368.8 9.0 copy-start.4
  377.8 109.3 %all-gather.11.cloned.1.call-start = ((), (), s32[]{:S(2)}) async-start(), calls=%async_computation.10 | async-start | bytes 3342336 | tf_op jit(solution)/shard_map/all_gather | solution.py:45
  378.4 190.8 %reduce-scatter.15.cloned.1.call-start = ((), (), s32[]{:S(2)}) async-start(), calls=%async_computation.11 | async-start | bytes 3342336 | tf_op jit(solution)/shard_map/reduce_scatter | solution.py:54
  410.2 410.0 %all-reduce.5.cloned.1.call-start = ((), (), s32[]{:S(2)}) async-start(), calls=%async_computation.12 | async-start | bytes 131072 | tf_op jit(solution)/shard_map/psum | solution.py:107
  509.0 68.4 %copy-start.27 = (s32[1,1,12]{2,1,0:T(1,128)S(1)}, s32[1,1,12]{2,1,0:T(1,128)}, u32[]{:S(2)}) copy-start(s32[1,1,12]{2,1,0:T(1,128)} %param.29) | copy-start | bytes 148
  573.2 6.0 copy-start.5
  573.2 6.0 copy-start.11
  580.8 508.0 %reduce-scatter.21.cloned.1.call-start = ((), (), s32[]{:S(2)}) async-start(), calls=%async_computation.17 | async-start | bytes 1671168 | tf_op jit(solution)/shard_map/reduce_scatter | solution.py:71
  847.6 178.0 %copy-start.25 = (s32[1,1,12]{2,1,0:T(1,128)S(1)}, s32[1,1,12]{2,1,0:T(1,128)}, u32[]{:S(2)}) copy-start(s32[1,1,12]{2,1,0:T(1,128)} %param.30) | copy-start | bytes 148
  936.4 87.8 %copy-start.9 = (f32[768,64]{0,1:T(8,128)}, f32[768,64]{0,1:T(8,128)S(1)}, u32[]{:S(2)}) copy-start(f32[768,64]{0,1:T(8,128)S(1)} %convolution_bitcast_fusion.13) | copy-start | bytes 589828
  1024.2 6.6 copy-start.6
  1030.8 107.3 %all-gather.13.cloned.1.call-start = ((), (), s32[]{:S(2)}) async-start(), calls=%async_computation.13 | async-start | bytes 3342336 | tf_op jit(solution)/shard_map/all_gather | solution.py:45
  1031.4 189.3 %reduce-scatter.17.cloned.1.call-start = ((), (), s32[]{:S(2)}) async-start(), calls=%async_computation.14 | async-start | bytes 3342336 | tf_op jit(solution)/shard_map/reduce_scatter | solution.py:54
  1063.0 405.5 %all-reduce.7.cloned.1.call-start = ((), (), s32[]{:S(2)}) async-start(), calls=%async_computation.15 | async-start | bytes 131072 | tf_op jit(solution)/shard_map/psum | solution.py:107
  1063.8 24.2 %copy-start.14 = (f32[768,64]{0,1:T(8,128)S(1)}, f32[768,64]{0,1:T(8,128)}, u32[]{:S(2)}) copy-start(f32[768,64]{0,1:T(8,128)} %fusion.42) | copy-start | bytes 589828
  1083.5 4.9 copy-start.15
  1083.5 5.4 copy-start.30
  1160.1 67.0 %copy-start.12 = (f32[12,64,64]{2,0,1:T(8,128)S(1)}, f32[12,64,64]{2,0,1:T(8,128)}, u32[]{:S(2)}) copy-start(f32[12,64,64]{2,0,1:T(8,128)} %fusion.36) | copy-start | bytes 589828
  1160.1 67.0 %copy-start.28 = (s32[1,1,12]{2,1,0:T(1,128)S(1)}, s32[1,1,12]{2,1,0:T(1,128)}, u32[]{:S(2)}) copy-start(s32[1,1,12]{2,1,0:T(1,128)} %param.29) | copy-start | bytes 148
  1222.8 5.2 copy-start.7
  1227.1 2.0 copy-start.10
Sparse Core Ops, SparseCore 0:
  11.7 43.3 all-gather.8
  57.6 53.5 reduce-scatter.12
  113.9 67.7 all-gather.6
  185.7 85.0 reduce-scatter.10
  377.9 52.2 reduce-scatter.18
  433.1 53.9 all-gather.10
  490.7 78.4 reduce-scatter.14
  580.9 239.1 all-reduce.4
  1030.9 50.4 reduce-scatter.20
  1084.0 54.0 all-gather.12
  1142.2 78.3 reduce-scatter.16
  1229.3 239.1 all-reduce.6
where the time goes:
time: 1590 us
  waiting for transfers between devices  751 us (47%)
  blocking collectives  497 us (31%)
  local copies, waits for them, and re-layouts  128 us (8%)
  matrix products  100 us (6%)
  other arithmetic  97.2 us (6%)
    psum x2, waiting for transfers between devices, local(): lax.psum((gram_product(basis, image_b), gram_product(basis, image_x)), ('...  321 us
    reduce_scatter x6, waiting for transfers between devices, apply_blocks(): lax.psum_scatter(jnp.einsum('bk,kiw->biw', chosen, backward, precision=pr...  253 us
    all_gather x3, waiting for transfers between devices, apply_blocks(): lax.all_gather(vector, 'row', axis=0, tiled=True).reshape(-1, KB, width)  162 us
    psum x2, blocking collectives, local(): lax.psum((gram_product(basis, image_b), gram_product(basis, image_x)), ('...  156 us
    psum x2, blocking collectives, project(): lax.psum((gram_product(current, current), gram_product(current, image_x))...  151 us
    psum x2, blocking collectives, local(): lengths = lax.psum(gram_product(moved, moved), ('sub', 'row'))  149 us
    all_gather x2, blocking collectives, apply_blocks(): lax.all_gather(boundary, 'sub', axis=0, tiled=True).reshape(-1, KB, width)  41.6 us
    another operation x12, other arithmetic, chol_solve(): factor = jnp.linalg.cholesky(matrix)  37.8 us
  transfers between devices with their start and end apart: 12, of which 10 were waited for; matrix products, arithmetic and copies ran while one was open for 11% of the time, Pallas kernels for 0%

commit v1 on v0

--- a/solution.py
+++ b/solution.py
@@ -8,6 +8,28 @@
 ITERS = 2
 IFR = 3
 precise_mode = lax.Precision.HIGHEST
+
+
+def joined_along(blocks, dim):
+    blocks = jnp.moveaxis(blocks, 0, dim)
+    dims = blocks.shape
+    return blocks.reshape(*dims[:dim], dims[dim] * dims[dim + 1], *dims[dim + 2 :])
+
+
+def gather_around(x, axis, dim):
+    devices = lax.axis_size(axis)
+    pairs = [(i, (i + 1) % devices) for i in range(devices)]
+    back = [(b, a) for a, b in pairs]
+    lower, upper = ([], [])
+    for hop in range(devices - 1):
+        if hop % 2 == 0:
+            lower.append(lax.ppermute(lower[-1] if lower else x, axis, pairs))
+        else:
+            upper.append(lax.ppermute(upper[-1] if upper else x, axis, back))
+    blocks = jnp.stack([*lower[::-1], x, *upper])
+    shift = lax.axis_index(axis) - len(lower)
+    blocks = blocks[(jnp.arange(devices) - shift) % devices]
+    return joined_along(blocks, dim)
 
 
 def gram_product(left, right):
@@ -61,7 +83,7 @@
     )
     result = result + returned.reshape(LB, KB, width)
     boundary = mine[bnd_here].reshape(-1, width)
-    remote = lax.all_gather(boundary, "sub", axis=0, tiled=True).reshape(-1, KB, width)
+    remote = gather_around(boundary, "sub", 0).reshape(-1, KB, width)
     forward = jnp.einsum("kij,kjw->kiw", face_vals, remote[face_src], precision=precise_mode)
     face_select = (face_rows[:, None] == local_ids[None, :]).astype(jnp.float32)
     result = result + jnp.einsum("ka,kiw->aiw", face_select, forward, precision=precise_mode)

time: 1590 us -> 1380 us (0.87)
  waiting for transfers between devices: 751 us -> 449 us
  starting transfers between devices: 1.4 us -> 94.3 us
  blocking collectives: 497 us -> 456 us
  local copies, waits for them, and re-layouts: 128 us -> 164 us
    all_gather x3, waiting for transfers between devices: 162 us -> 0.03 us  [apply_blocks(): lax.all_gather(vector, 'row', axis=0, tiled=True).reshape(-1, KB, width)]
    reduce_scatter x6, waiting for transfers between devices: 253 us -> 101 us  [apply_blocks(): lax.psum_scatter(jnp.einsum('bk,kiw->biw', chosen, backward, precision=pr...]
    ppermute x0 -> x45, starting transfers between devices: none -> 92.6 us  [the longest x21 66.5 us: gather_around(): upper.append(lax.ppermute(upper[-1] if upper else x, axis, back))]
    all_gather x2 -> x0, blocking collectives: 41.6 us -> none  [apply_blocks(): lax.all_gather(boundary, 'sub', axis=0, tiled=True).reshape(-1, KB, width)]
    unnamed x69 -> x122, local copies, waits for them, and re-layouts: 8.94 us -> 38.8 us
    ppermute x0 -> x45, waiting for transfers between devices: none -> 26 us  [the longest x24 13.5 us: gather_around(): lower.append(lax.ppermute(lower[-1] if lower else x, axis, pairs))]
  transfers between devices with their start and end apart: 12 -> 56, of which waited for: 10 -> 36; matrix products, arithmetic and copies ran while one was open for 11% -> 15% of each run, Pallas kernels for 0% -> 0%
where the time goes in v1:
time: 1380 us
  blocking collectives  456 us (33%)
  waiting for transfers between devices  449 us (33%)
  local copies, waits for them, and re-layouts  164 us (12%)
  matrix products  97.9 us (7%)
  other arithmetic  97.3 us (7%)
  starting transfers between devices  94.3 us (7%)
  between operations  17.3 us (1%)
    psum x2, waiting for transfers between devices, local(): lax.psum((gram_product(basis, image_b), gram_product(basis, image_x)), ('...  320 us
    psum x2, blocking collectives, local(): lax.psum((gram_product(basis, image_b), gram_product(basis, image_x)), ('...  156 us
    psum x2, blocking collectives, project(): lax.psum((gram_product(current, current), gram_product(current, image_x))...  151 us
    psum x2, blocking collectives, local(): lengths = lax.psum(gram_product(moved, moved), ('sub', 'row'))  149 us
    reduce_scatter x6, waiting for transfers between devices, apply_blocks(): lax.psum_scatter(jnp.einsum('bk,kiw->biw', chosen, backward, precision=pr...  101 us
    ppermute x21, starting transfers between devices, gather_around(): upper.append(lax.ppermute(upper[-1] if upper else x, axis, back))  66.5 us
    unnamed x122, local copies, waits for them, and re-layouts  38.8 us
    another operation x12, other arithmetic, chol_solve(): factor = jnp.linalg.cholesky(matrix)  37.8 us
  transfers between devices with their start and end apart: 56, of which 36 were waited for; matrix products, arithmetic and copies ran while one was open for 15% of the time, Pallas kernels for 0%

profile of v1, /device:TPU:1, one launch (start us, length us, event | category | flops | bytes accessed | tf_op | source)
XLA Modules:
  0.0 1376.4 jit_solution(3034359646065218790)
XLA Ops:
  26.1 4.6 fusion
  30.7 6.3 copy.146
  72.7 4.8 collective-permute-start.13
  78.5 4.8 collective-permute-start.14
  100.8 5.2 gather_fusion
  106.0 5.4 convolution_bitcast_fusion.2
  111.4 56.3 %reduce-scatter.11.cloned.1.call-done = f32[768,128]{1,0:T(8,128)} async-done(((f32[12288,128]{1,0:T(8,128)}), f32[768,128]{1,0:T(8,128)}) %reduce-scatter.11.cloned.1.call-update) | async-done | bytes 393232 | tf_op jit(solution)/shard_map/reduce_scatter | solution.py:76
  167.8 4.8 fusion.7
  174.3 76.9 %all-reduce.1 = (f32[64,64]{0,1:T(8,128)S(1)}, f32[64,64]{0,1:T(8,128)S(1)}) all-reduce(f32[64,64]{0,1:T(8,128)S(1)} %convolution_bitcast_fusion.16, f32[64,64]{0,1:T(8,128)S(1)} %copy-done.19), channel_id=1, replica_groups=mesh['sub'=16,'row'=16] {'sub','row'}, use_global_device_ids=true, to_apply=%region_5.7 | all-reduce | flops 8192 | bytes 65536 | tf_op jit(solution)/shard_map/psum | solution.py:56
  251.4 5.8 cholesky.116
  258.6 4.9 custom-call.29
  278.2 6.5 multiply_bitcast_fusion.1
  284.7 4.7 copy.164
  289.4 5.5 fusion.44
  294.9 6.4 copy.165
  301.3 5.9 reshape.332
  367.2 5.8 copy.231
  373.0 5.4 gather_fusion.6
  378.4 6.2 convolution_bitcast_fusion.1
  384.6 4.7 copy.160
  389.3 22.6 %reduce-scatter.15.cloned.1.call-done = f32[768,64]{0,1:T(8,128)} async-done(((f32[12288,64]{0,1:T(8,128)}), f32[768,64]{0,1:T(8,128)}) %reduce-scatter.15.cloned.1.call-update) | async-done | bytes 196624 | tf_op jit(solution)/shard_map/reduce_scatter | solution.py:76
  424.3 78.0 %psum.73 = f32[128,64]{0,1:T(8,128)S(1)} all-reduce(f32[128,64]{0,1:T(8,128)} %fusion.27), channel_id=1, replica_groups=mesh['sub'=16,'row'=16] {'sub','row'}, use_global_device_ids=true, to_apply=%region_11.0 | all-reduce | flops 8192 | bytes 65536 | tf_op jit(solution)/shard_map/psum | solution.py:129
  502.2 159.5 %all-reduce.5.cloned.1.call-done = f32[128,128]{0,1:T(8,128)} async-done(((f32[128,128]{0,1:T(8,128)}), f32[128,128]{0,1:T(8,128)}) %all-reduce.5.cloned.1.call-update) | async-done | bytes 65552 | tf_op jit(solution)/shard_map/psum | solution.py:129
  663.5 11.7 cholesky.127
  676.6 9.8 custom-call.31
  689.5 74.6 %psum.74 = f32[64,64]{0,1:T(8,128)S(1)} all-reduce(f32[64,64]{0,1:T(8,128)S(1)} %fusion.133), channel_id=1, replica_groups=mesh['sub'=16,'row'=16] {'sub','row'}, use_global_device_ids=true, to_apply=%region_12.19 | all-reduce | flops 4096 | bytes 32768 | tf_op jit(solution)/shard_map/psum | solution.py:137
  764.2 5.8 cholesky.138
  771.3 4.9 custom-call.32
  777.7 74.2 %all-reduce = (f32[64,64]{1,0:T(8,128)S(1)}, f32[64,64]{0,1:T(8,128)S(1)}) all-reduce(f32[64,64]{1,0:T(8,128)S(1)} %fusion.135, f32[64,64]{0,1:T(8,128)S(1)} %fusion.134), channel_id=1, replica_groups=mesh['sub'=16,'row'=16] {'sub','row'}, use_global_device_ids=true, to_apply=%region_14.22 | all-reduce | flops 8192 | bytes 65536 | tf_op jit(solution)/shard_map/psum | solution.py:56
  852.0 5.8 cholesky.149
  859.2 4.9 custom-call.35
  874.8 6.6 multiply_bitcast_fusion
  881.4 4.7 copy.193
  886.1 5.5 fusion.43
  891.6 6.4 copy.194
  898.0 5.9 reshape.340
  962.6 5.8 copy.235
  968.4 5.4 gather_fusion.12
  973.8 6.2 convolution_bitcast_fusion
  980.1 4.7 copy.189
  984.7 22.4 %reduce-scatter.17.cloned.1.call-done = f32[768,64]{0,1:T(8,128)} async-done(((f32[12288,64]{0,1:T(8,128)}), f32[768,64]{0,1:T(8,128)}) %reduce-scatter.17.cloned.1.call-update) | async-done | bytes 196624 | tf_op jit(solution)/shard_map/reduce_scatter | solution.py:76
  1015.4 77.7 %psum.78 = f32[128,64]{0,1:T(8,128)S(1)} all-reduce(f32[128,64]{0,1:T(8,128)S(1)} %fusion.25), channel_id=1, replica_groups=mesh['sub'=16,'row'=16] {'sub','row'}, use_global_device_ids=true, to_apply=%region_18.26 | all-reduce | flops 8192 | bytes 65536 | tf_op jit(solution)/shard_map/psum | solution.py:129
  1093.1 160.6 %all-reduce.7.cloned.1.call-done = f32[128,128]{0,1:T(8,128)} async-done(((f32[128,128]{0,1:T(8,128)}), f32[128,128]{0,1:T(8,128)}) %all-reduce.7.cloned.1.call-update) | async-done | bytes 65552 | tf_op jit(solution)/shard_map/psum | solution.py:129
  1255.5 11.7 cholesky.160
  1268.5 9.8 custom-call.39
  1279.5 74.6 %psum.79 = f32[64,64]{0,1:T(8,128)S(1)} all-reduce(f32[64,64]{0,1:T(8,128)S(1)} %fusion.136), channel_id=1, replica_groups=mesh['sub'=16,'row'=16] {'sub','row'}, use_global_device_ids=true, to_apply=%region_19.27 | all-reduce | flops 4096 | bytes 32768 | tf_op jit(solution)/shard_map/psum | solution.py:137
  1354.2 5.8 cholesky.171
  1361.4 4.9 custom-call.40
  (363 shorter events, 257.5 us)
Async XLA Ops:
  8.0 91.3 %reduce-scatter.13.cloned.1.call-start = ((), (), s32[]{:S(2)}) async-start(), calls=%async_computation.8 | async-start | bytes 1671168 | tf_op jit(solution)/shard_map/reduce_scatter | solution.py:93
  16.1 84.7 %all-gather.4.cloned.1.call-start = ((), (), s32[]{:S(2)}) async-start(), calls=%async_computation.6 | async-start | bytes 6684672 | tf_op jit(solution)/shard_map/all_gather | solution.py:67
  16.6 151.1 %reduce-scatter.11.cloned.1.call-start = ((), (), s32[]{:S(2)}) async-start(), calls=%async_computation.7 | async-start | bytes 6684672 | tf_op jit(solution)/shard_map/reduce_scatter | solution.py:76
  37.0 327.9 %reduce-scatter.19.cloned.1.call-start = ((), (), s32[]{:S(2)}) async-start(), calls=%async_computation.15 | async-start | bytes 1671168 | tf_op jit(solution)/shard_map/reduce_scatter | solution.py:93
  38.1 4.7 collective-permute-start
  42.8 5.2 collective-permute-start.1
  45.2 5.0 collective-permute-start.8
  48.0 5.3 collective-permute-start.2
  50.1 4.8 collective-permute-start.9
  53.2 5.4 collective-permute-start.3
  55.0 7.0 collective-permute-start.10
  58.6 7.9 collective-permute-start.4
  62.0 5.5 collective-permute-start.11
  66.6 5.2 collective-permute-start.5
  67.5 5.2 collective-permute-start.12
  71.7 5.8 collective-permute-start.6
  72.7 5.8 collective-permute-start.13
  77.5 5.7 collective-permute-start.7
  78.5 14.4 %collective-permute-start.14 = (f32[192,128]{1,0:T(8,128)S(1)}, f32[192,128]{1,0:T(8,128)S(1)}, u32[]{:S(2)}, u32[]{:S(2)}) collective-permute-start(f32[192,128]{1,0:T(8,128)S(1)} %collective-permute-done.13), channel_id=1, source_target_pairs={{16,0},{32,16},{48,32},{64,48},{80,64},{96,80},{112,96},{128,112},... | collective-permute-start | bytes 294920 | tf_op jit(solution)/shard_map/ppermute | solution.py:28
  274.8 92.3 %all-gather.6.cloned.1.call-start = ((), (), s32[]{:S(2)}) async-start(), calls=%async_computation.9 | async-start | bytes 3342336 | tf_op jit(solution)/shard_map/all_gather | solution.py:67
  275.4 136.5 %reduce-scatter.15.cloned.1.call-start = ((), (), s32[]{:S(2)}) async-start(), calls=%async_computation.10 | async-start | bytes 3342336 | tf_op jit(solution)/shard_map/reduce_scatter | solution.py:76
  307.1 354.6 %all-reduce.5.cloned.1.call-start = ((), (), s32[]{:S(2)}) async-start(), calls=%async_computation.11 | async-start | bytes 131072 | tf_op jit(solution)/shard_map/psum | solution.py:129
  313.9 4.9 collective-permute-start.23
  315.7 5.0 collective-permute-start.17
  318.8 4.8 collective-permute-start.24
  320.7 5.5 collective-permute-start.18
  326.2 5.6 collective-permute-start.19
  331.9 5.3 collective-permute-start.20
  332.3 5.3 collective-permute-start.27
  337.1 5.3 collective-permute-start.21
  337.6 5.3 collective-permute-start.28
  342.4 5.3 collective-permute-start.22
  342.8 14.4 %collective-permute-start.29 = (f32[192,64]{1,0:T(8,128)S(1)}, f32[192,64]{1,0:T(8,128)S(1)}, u32[]{:S(2)}, u32[]{:S(2)}) collective-permute-start(f32[192,64]{1,0:T(8,128)S(1)} %collective-permute-done.28), channel_id=1, source_target_pairs={{16,0},{32,16},{48,32},{64,48},{80,64},{96,80},{112,96},{128,112},... | collective-permute-start | bytes 147464 | tf_op jit(solution)/shard_map/ppermute | solution.py:28
  422.8 537.5 %reduce-scatter.21.cloned.1.call-start = ((), (), s32[]{:S(2)}) async-start(), calls=%async_computation.16 | async-start | bytes 1671168 | tf_op jit(solution)/shard_map/reduce_scatter | solution.py:93
  871.5 91.1 %all-gather.8.cloned.1.call-start = ((), (), s32[]{:S(2)}) async-start(), calls=%async_computation.12 | async-start | bytes 3342336 | tf_op jit(solution)/shard_map/all_gather | solution.py:67
  872.3 134.9 %reduce-scatter.17.cloned.1.call-start = ((), (), s32[]{:S(2)}) async-start(), calls=%async_computation.13 | async-start | bytes 3342336 | tf_op jit(solution)/shard_map/reduce_scatter | solution.py:76
  903.9 349.8 %all-reduce.7.cloned.1.call-start = ((), (), s32[]{:S(2)}) async-start(), calls=%async_computation.14 | async-start | bytes 131072 | tf_op jit(solution)/shard_map/psum | solution.py:129
  910.7 4.6 collective-permute-start.38
  915.3 4.7 collective-permute-start.39
  916.8 5.5 collective-permute-start.33
  922.3 5.7 collective-permute-start.34
  924.4 4.5 collective-permute-start.41
  928.0 5.3 collective-permute-start.35
  929.0 5.3 collective-permute-start.42
  933.3 5.3 collective-permute-start.36
  934.2 5.3 collective-permute-start.43
  938.6 5.3 collective-permute-start.37
  939.5 13.9 %collective-permute-start.44 = (f32[192,64]{1,0:T(8,128)S(1)}, f32[192,64]{1,0:T(8,128)S(1)}, u32[]{:S(2)}, u32[]{:S(2)}) collective-permute-start(f32[192,64]{1,0:T(8,128)S(1)} %collective-permute-done.43), channel_id=1, source_target_pairs={{16,0},{32,16},{48,32},{64,48},{80,64},{96,80},{112,96},{128,112},... | collective-permute-start | bytes 147464 | tf_op jit(solution)/shard_map/ppermute | solution.py:28
  (44 other events, 696.7 us)
Sparse Core Ops, SparseCore 0:
  16.2 60.6 reduce-scatter.12
  81.0 86.6 reduce-scatter.10
  275.0 52.7 reduce-scatter.18
  331.2 80.6 reduce-scatter.14
  871.6 50.9 reduce-scatter.20
  926.6 80.5 reduce-scatter.16
Sparse Core Ops, SparseCore 1:
  19.3 69.8 all-gather.3
  278.6 48.7 all-gather.5
  422.9 238.8 all-reduce.4
  875.3 47.0 all-gather.7
  1015.0 238.7 all-reduce.6
